TPU v7x, 32 devices: a whole 2x2x4 slice. The times are simulated.
32 devices in a mesh: seq: 16 (over z, y, x), ch: 2 (over core).
Axes of the slice: x: 2, y: 2, z: 4, core: 2. Of those that a mesh axis runs over, the one named last changes fastest.
Arguments:
- query: bfloat16 [4096, 4096], P('seq', 'ch'), may hold values from -6 to 6
- key_in: bfloat16 [4096, 4096], P('seq', 'ch'), may hold values from -6 to 6
- values: bfloat16 [4096, 4096], P('seq', 'ch'), may hold values from -6 to 6
- cotangent: bfloat16 [4096, 4096], P('seq', 'ch'), may hold values from -6 to 6
- residues: float32 [16, 128], replicated, may hold values from -1.5 to 1.5
- decay_rates: float32 [16, 128], replicated, may hold values from 0.00012207031 to 0.1
Outputs:
- query_grad: bfloat16 [4096, 4096], P('seq', 'ch')
- key_grad: bfloat16 [4096, 4096], P('seq', 'ch')
- value_grad: bfloat16 [4096, 4096], P('seq', 'ch')
- residue_grad: float32 [16, 128], replicated
- rate_grad: float32 [16, 128], replicated
All inputs are finite; a program needn't handle non-finite values.
Results may differ from a plain program's by a relative error of at most 0.0012.
Values sent between devices are 32-bit elements; how exact they have to be, the bound alone decides.
A program may use at most 128 MiB of HBM per device.

v0:
```python
import math

import jax
import jax.numpy as jnp
from jax import lax
from jax.sharding import PartitionSpec as P

highest = lax.Precision.HIGHEST


def unit_angles(first_ids, second_ids, modulus):
    product = first_ids[:, None] * second_ids[None, :] % modulus
    angle = product.astype(jnp.float32) * (2.0 * math.pi / modulus)
    return (jnp.cos(angle), jnp.sin(angle))


def contract(table, field, form):
    return jnp.einsum(form, table, field, precision=highest)


def block_forward(blocks, row_ids, padded):
    count = blocks.shape[0]
    freq_ids = jnp.arange(2 * count, dtype=jnp.int32)
    cosine, sine = unit_angles(freq_ids, jnp.arange(count, dtype=jnp.int32), 2 * count)
    real_part = contract(cosine, blocks, "ka,arc->krc")
    imag_part = -contract(sine, blocks, "ka,arc->krc")
    cos_twist, sin_twist = unit_angles(freq_ids, row_ids, padded)
    cos_twist = cos_twist[:, :, None]
    sin_twist = sin_twist[:, :, None]
    return (
        real_part * cos_twist + imag_part * sin_twist,
        imag_part * cos_twist - real_part * sin_twist,
    )


def row_forward(real_part, imag_part):
    row_ids = jnp.arange(real_part.shape[1], dtype=jnp.int32)
    cosine, sine = unit_angles(row_ids, row_ids, real_part.shape[1])
    new_real = contract(cosine, real_part, "sr,krc->ksc") + contract(sine, imag_part, "sr,krc->ksc")
    new_imag = contract(cosine, imag_part, "sr,krc->ksc") - contract(sine, real_part, "sr,krc->ksc")
    return (new_real, new_imag)


def row_inverse(real_part, imag_part, freq_ids, padded):
    row_ids = jnp.arange(real_part.shape[1], dtype=jnp.int32)
    cosine, sine = unit_angles(row_ids, row_ids, real_part.shape[1])
    new_real = contract(cosine, real_part, "sr,krc->ksc") - contract(sine, imag_part, "sr,krc->ksc")
    new_imag = contract(cosine, imag_part, "sr,krc->ksc") + contract(sine, real_part, "sr,krc->ksc")
    cos_twist, sin_twist = unit_angles(freq_ids, row_ids, padded)
    cos_twist = cos_twist[:, :, None]
    sin_twist = sin_twist[:, :, None]
    return (
        new_real * cos_twist - new_imag * sin_twist,
        new_imag * cos_twist + new_real * sin_twist,
    )


def block_inverse(real_part, imag_part, count, padded):
    freq_count = real_part.shape[0]
    cosine, sine = unit_angles(
        jnp.arange(count, dtype=jnp.int32), jnp.arange(freq_count, dtype=jnp.int32), freq_count
    )
    return (
        contract(cosine, real_part, "ak,krc->arc") - contract(sine, imag_part, "ak,krc->arc")
    ) / padded


def mode_scale(decay_rates):
    return jnp.sqrt(-jnp.expm1(-2.0 * decay_rates))


def filter_time(residues, decay_rates, positions):
    scale = mode_scale(decay_rates)
    impulse = jnp.zeros((positions.shape[0], residues.shape[1]), jnp.float32)
    for mode_index in range(residues.shape[0]):
        impulse = impulse + (residues[mode_index] * scale[mode_index])[None, :] * jnp.exp(
            -decay_rates[mode_index][None, :] * positions[:, None]
        )
    return impulse


def spectral_products(gate_re, gate_im, sig_re, sig_im, filt_re, filt_im, groups):
    shape = gate_re.shape
    split = shape[:2] + (groups, shape[2] // groups)
    gate_re = gate_re.reshape(split)
    gate_im = gate_im.reshape(split)
    sig_re = sig_re.reshape(split)
    sig_im = sig_im.reshape(split)
    filt_re = filt_re[:, :, None, :]
    filt_im = filt_im[:, :, None, :]
    conv_re = (gate_re * filt_re - gate_im * filt_im).reshape(shape)
    conv_im = (gate_re * filt_im + gate_im * filt_re).reshape(shape)
    back_re = (sig_re * filt_re + sig_im * filt_im).reshape(shape)
    back_im = (sig_im * filt_re - sig_re * filt_im).reshape(shape)
    corr_re = jnp.sum(sig_re * gate_re + sig_im * gate_im, axis=2)
    corr_im = jnp.sum(sig_im * gate_re - sig_re * gate_im, axis=2)
    return (conv_re, conv_im, back_re, back_im, corr_re, corr_im)


def filter_sums(filter_grad, residues, decay_rates, positions):
    scale = mode_scale(decay_rates)
    slope = jnp.exp(-2.0 * decay_rates) / scale
    firsts = []
    seconds = []
    for mode_index in range(residues.shape[0]):
        weighted = filter_grad * jnp.exp(-decay_rates[mode_index][None, :] * positions[:, None])
        firsts.append(scale[mode_index] * jnp.sum(weighted, axis=0))
        factor = slope[mode_index][None, :] - scale[mode_index][None, :] * positions[:, None]
        seconds.append(
            decay_rates[mode_index] * residues[mode_index] * jnp.sum(weighted * factor, axis=0)
        )
    return (jnp.stack(firsts), jnp.stack(seconds))


def shards(query, key_in, values, cotangent, residues, decay_rates):
    seq_devices = lax.axis_size("seq")
    seq_index = lax.axis_index("seq")
    row_count, channels = query.shape
    filters = residues.shape[1]
    groups = channels // filters
    length = seq_devices * row_count
    padded = 2 * length
    gated = key_in.astype(jnp.float32) * values.astype(jnp.float32)
    signal_grad = cotangent.astype(jnp.float32) * query.astype(jnp.float32)
    row_ids = jnp.arange(row_count, dtype=jnp.int32)
    positions = (seq_index * row_count + row_ids).astype(jnp.float32)
    piece_rows = row_count // seq_devices
    own_freq = 2 * seq_index + jnp.arange(2, dtype=jnp.int32)
    stacked = jnp.concatenate(
        [gated, signal_grad, filter_time(residues, decay_rates, positions)], axis=1
    )
    blocks = lax.all_to_all(stacked[None], "seq", split_axis=1, concat_axis=0, tiled=True)
    own_rows = seq_index * piece_rows + jnp.arange(piece_rows, dtype=jnp.int32)
    real_part, imag_part = block_forward(blocks, own_rows, padded)
    real_part, imag_part = (
        lax.all_to_all(real_part, "seq", split_axis=0, concat_axis=1, tiled=True),
        lax.all_to_all(imag_part, "seq", split_axis=0, concat_axis=1, tiled=True),
    )
    real_part, imag_part = row_forward(real_part, imag_part)
    gate_re = real_part[..., :channels]
    gate_im = imag_part[..., :channels]
    sig_re = real_part[..., channels : 2 * channels]
    sig_im = imag_part[..., channels : 2 * channels]
    filt_re = real_part[..., 2 * channels :]
    filt_im = imag_part[..., 2 * channels :]
    conv_re, conv_im, back_re, back_im, corr_re, corr_im = spectral_products(
        gate_re, gate_im, sig_re, sig_im, filt_re, filt_im, groups
    )
    spec_re = jnp.concatenate([conv_re, back_re, corr_re], axis=2)
    spec_im = jnp.concatenate([conv_im, back_im, corr_im], axis=2)
    inner_re, inner_im = row_inverse(spec_re, spec_im, own_freq, padded)
    moved_re, moved_im = (
        lax.all_to_all(inner_re, "seq", split_axis=1, concat_axis=0, tiled=True),
        lax.all_to_all(inner_im, "seq", split_axis=1, concat_axis=0, tiled=True),
    )
    time_re = block_inverse(moved_re, moved_im, seq_devices, padded)
    rows_re = lax.all_to_all(time_re, "seq", split_axis=0, concat_axis=1, tiled=True)
    conv = rows_re[0, :, :channels]
    gated_grad = rows_re[0, :, channels : 2 * channels]
    filter_grad = rows_re[0, :, 2 * channels :]
    firsts, seconds = filter_sums(filter_grad, residues, decay_rates, positions)
    firsts, seconds = lax.psum((firsts, seconds), ("seq", "ch"))
    norm_factor = 1.0 / math.sqrt(length)
    query_grad = (cotangent.astype(jnp.float32) * conv).astype(jnp.bfloat16)
    key_grad = (gated_grad * values.astype(jnp.float32)).astype(jnp.bfloat16)
    value_grad = (gated_grad * key_in.astype(jnp.float32)).astype(jnp.bfloat16)
    return (query_grad, key_grad, value_grad, firsts * norm_factor, seconds * norm_factor)


def solution(mesh):
    in_specs = (P("seq", "ch"), P("seq", "ch"), P("seq", "ch"), P("seq", "ch"), P(), P())
    out_specs = (P("seq", "ch"), P("seq", "ch"), P("seq", "ch"), P(), P())
    return jax.shard_map(shards, mesh=mesh, in_specs=in_specs, out_specs=out_specs, check_vma=False)
```

profile of v0, /device:TPU:0, one launch (start us, length us, event | category | flops | bytes accessed | tf_op | source)
XLA Modules:
  0.0 1282.7 jit_solution(11088856515414507532)
XLA Ops:
  1.8 1.3 exponential_divide_fusion
  3.2 1.4 slice_bitcast_fusion.31
  5.6 3.0 convert_multiply_fusion.1
  9.5 6.5 copy.44
  15.9 8.7 all-to-all-start
  24.7 82.0 %all-to-all-done = f32[1,256,4224]{2,0,1:T(1,128)} async-done(((f32[1,256,4224]{2,0,1:T(1,128)}), f32[1,256,4224]{2,0,1:T(1,128)}, u32[]{:S(2)}, u32[]{:S(2)}) %all-to-all-start) | async-done | bytes 4325408 | tf_op jit(solution)/shard_map/all_to_all | solution.py:132
  106.7 2.5 copy.66
  109.2 8.0 fusion.8
  117.2 12.3 multiply_add_fusion
  129.5 8.3 copy.47
  137.9 20.6 %all-to-all-start.1 = ((f32[32,16,4224]{2,1,0:T(8,128)}), f32[32,16,4224]{2,1,0:T(8,128)}, u32[]{:S(2)}, u32[]{:S(2)}) async-start(f32[32,16,4224]{2,1,0:T(8,128)} %copy.47), calls=%async_computation.1 | async-start | bytes 17301504 | tf_op jit(solution)/shard_map/all_to_all | solution.py:136
  158.5 11.8 copy.50
  170.3 147.7 %all-to-all-done.1 = f32[32,16,4224]{2,1,0:T(8,128)} async-done(((f32[32,16,4224]{2,1,0:T(8,128)}), f32[32,16,4224]{2,1,0:T(8,128)}, u32[]{:S(2)}, u32[]{:S(2)}) %all-to-all-start.1) | async-done | bytes 8650784 | tf_op jit(solution)/shard_map/all_to_all | solution.py:136
  318.0 40.8 %all-to-all-start.2 = ((f32[32,16,4224]{2,1,0:T(8,128)}), f32[32,16,4224]{2,1,0:T(8,128)}, u32[]{:S(2)}, u32[]{:S(2)}) async-start(f32[32,16,4224]{2,1,0:T(8,128)} %copy.50), calls=%async_computation.2 | async-start | bytes 17301504 | tf_op jit(solution)/shard_map/all_to_all | solution.py:137
  359.0 4.0 copy.48
  363.0 3.3 copy-done
  366.3 18.6 %fusion.24 = f32[2,4224,256]{2,1,0:T(8,128)} fusion(f32[2,256,4224]{2,1,0:T(8,128)S(1)} %bitcast.366), kind=kOutput, calls=%fused_computation.57 | convolution fusion | flops 6644695040 | bytes 17301504 | tf_op jit(solution)/shard_map/sr,krc->ksc/dot_general | solution.py:18
  384.9 130.6 %all-to-all-done.2 = f32[32,16,4224]{2,1,0:T(8,128)} async-done(((f32[32,16,4224]{2,1,0:T(8,128)}), f32[32,16,4224]{2,1,0:T(8,128)}, u32[]{:S(2)}, u32[]{:S(2)}) %all-to-all-start.2) | async-done | bytes 8650784 | tf_op jit(solution)/shard_map/all_to_all | solution.py:137
  515.5 4.1 copy.51
  519.6 17.7 %fusion.22 = f32[2,4224,256]{2,1,0:T(8,128)} fusion(f32[2,256,4224]{2,1,0:T(8,128)S(1)} %bitcast.370), kind=kOutput, calls=%fused_computation.55 | convolution fusion | flops 6644695040 | bytes 17301504 | tf_op jit(solution)/shard_map/sr,krc->ksc/dot_general | solution.py:18
  537.3 21.1 %add_bitcast_fusion.1 = f32[2,256,4224]{1,2,0:T(8,128)} fusion(f32[2,4224,256]{2,1,0:T(8,128)} %fusion.24, f32[2,256,4224]{2,1,0:T(8,128)S(1)} %bitcast.371), kind=kOutput, calls=%fused_computation.13 | convolution fusion | flops 6646857728 | bytes 25952256 | tf_op jit(solution)/shard_map/sr,krc->ksc/dot_general | solution.py:18
  558.5 20.9 %subtract_bitcast_fusion.1 = f32[2,256,4224]{1,2,0:T(8,128)} fusion(f32[2,4224,256]{2,1,0:T(8,128)} %fusion.22, f32[2,256,4224]{2,1,0:T(8,128)S(1)} %bitcast.369), kind=kOutput, calls=%fused_computation.12 | convolution fusion | flops 6646857728 | bytes 25952256 | tf_op jit(solution)/shard_map/sr,krc->ksc/dot_general | solution.py:18
  580.4 11.0 fusion.3
  591.4 2.5 reduce_sum.370
  593.8 2.5 reduce_sum.371
  596.3 13.4 %fusion.2 = f32[2,4224,256]{2,1,0:T(8,128)} fusion(f32[2,256,128]{1,2,0:T(8,128)S(1)} %reduce_sum.370, f32[2,256,2048]{1,2,0:T(8,128)} %get-tuple-element.62, f32[2,256,2048]{1,2,0:T(8,128)} %get-tuple-element.59), kind=kOutput, calls=%fused_computation.22 | convolution fusion | flops 6649020416 | bytes 17301504 | tf_op jit(solution)/shard_map/sr,krc->ksc/dot_general | solution.py:18
  609.8 13.3 %fusion.1 = f32[2,4224,256]{2,1,0:T(8,128)} fusion(f32[2,256,128]{1,2,0:T(8,128)S(1)} %reduce_sum.371, f32[2,256,2048]{1,2,0:T(8,128)S(1)} %copy-done.2, f32[2,256,2048]{1,2,0:T(8,128)S(1)} %copy-done.1), kind=kOutput, calls=%fused_computation.21 | convolution fusion | flops 6649020416 | bytes 17301504 | tf_op jit(solution)/shard_map/sr,krc->ksc/dot_general | solution.py:18
  623.1 15.2 %convolution_add_fusion = f32[2,4224,256]{2,1,0:T(8,128)} fusion(f32[2,4224,256]{2,1,0:T(8,128)} %fusion.1, f32[2,256,128]{1,2,0:T(8,128)S(1)} %reduce_sum.370, f32[2,256,2048]{1,2,0:T(8,128)S(1)} %copy-done.4, f32[2,256,2048]{1,2,0:T(8,128)S(1)} %copy-done.3), kind=kOutput, calls=%fused_computation.16 | convolution fusion | flops 6651183104 | bytes 25952256 | tf_op jit(solution)/shard_map/sr,krc->ksc/dot_general | solution.py:18
  638.3 18.5 %add_bitcast_fusion = (f32[2,256,4224]{1,2,0:T(8,128)}, f32[2,256,4224]{1,2,0:T(8,128)}) fusion(f32[2,4224,256]{2,1,0:T(8,128)} %convolution_add_fusion, f32[2,256]{1,0:T(2,128)S(1)} %get-tuple-element.184, f32[2,256]{1,0:T(2,128)S(1)} %get-tuple-element.183, f32[2,4224,256]{2,1,0:T(8,128)} %fusion.2, f32[2,256,128]{1,2,0:T(8,128)S(1)} %reduce_sum.371, ...), kind=kOutput, calls=%fused_computation.10 | convolution fusion | flops 6664159232 | bytes 43257856 | tf_op jit(solution)/shard_map/sr,krc->ksc/dot_general | solution.py:18
  656.8 14.0 %copy.55 = f32[2,256,4224]{2,0,1:T(2,128)} copy(f32[2,256,4224]{1,2,0:T(8,128)} %get-tuple-element.66) | data formatting | bytes 17301504 | tf_op jit(solution)/shard_map/sub | solution.py:53
  670.8 38.6 %all-to-all-start.3 = ((f32[2,256,4224]{2,0,1:T(2,128)}), f32[2,256,4224]{2,0,1:T(2,128)}, u32[]{:S(2)}, u32[]{:S(2)}) async-start(f32[2,256,4224]{2,0,1:T(2,128)} %copy.55), calls=%async_computation.3 | async-start | bytes 17301504 | tf_op jit(solution)/shard_map/all_to_all | solution.py:153
  709.4 13.9 %copy.58 = f32[2,256,4224]{2,0,1:T(2,128)} copy(f32[2,256,4224]{1,2,0:T(8,128)} %get-tuple-element.65) | data formatting | bytes 17301504 | tf_op jit(solution)/shard_map/add | solution.py:54
  723.4 144.0 %all-to-all-done.3 = f32[2,256,4224]{2,0,1:T(2,128)} async-done(((f32[2,256,4224]{2,0,1:T(2,128)}), f32[2,256,4224]{2,0,1:T(2,128)}, u32[]{:S(2)}, u32[]{:S(2)}) %all-to-all-start.3) | async-done | bytes 8650784 | tf_op jit(solution)/shard_map/all_to_all | solution.py:153
  867.3 40.0 %all-to-all-start.4 = ((f32[2,256,4224]{2,0,1:T(2,128)}), f32[2,256,4224]{2,0,1:T(2,128)}, u32[]{:S(2)}, u32[]{:S(2)}) async-start(f32[2,256,4224]{2,0,1:T(2,128)} %copy.58), calls=%async_computation.4 | async-start | bytes 17301504 | tf_op jit(solution)/shard_map/all_to_all | solution.py:154
  907.3 4.0 copy.56
  911.3 8.2 copy.57
  919.5 11.2 all_to_all.83
  930.7 8.1 fusion.83
  938.7 123.6 %all-to-all-done.4 = f32[2,256,4224]{2,0,1:T(2,128)} async-done(((f32[2,256,4224]{2,0,1:T(2,128)}), f32[2,256,4224]{2,0,1:T(2,128)}, u32[]{:S(2)}, u32[]{:S(2)}) %all-to-all-start.4) | async-done | bytes 8650784 | tf_op jit(solution)/shard_map/all_to_all | solution.py:154
  1062.3 4.0 copy.59
  1066.3 8.3 copy.60
  1074.6 11.1 all_to_all.87
  1085.8 7.7 fusion
  1093.5 3.3 copy.61
  1097.0 38.2 %all-to-all-start.5 = ((f32[16,16,4224]{2,1,0:T(8,128)}), f32[16,16,4224]{2,1,0:T(8,128)}, u32[]{:S(2)}, u32[]{:S(2)}) async-start(f32[16,16,4224]{2,1,0:T(8,128)} %copy.61), calls=%async_computation.5 | async-start | bytes 8650752 | tf_op jit(solution)/shard_map/all_to_all | solution.py:157
  1135.2 80.6 %all-to-all-done.5 = f32[16,16,4224]{2,1,0:T(8,128)} async-done(((f32[16,16,4224]{2,1,0:T(8,128)}), f32[16,16,4224]{2,1,0:T(8,128)}, u32[]{:S(2)}, u32[]{:S(2)}) %all-to-all-start.5) | async-done | bytes 4325408 | tf_op jit(solution)/shard_map/all_to_all | solution.py:157
  1215.9 4.5 fusion.11
  1226.4 54.9 %all-reduce = (f32[16,128]{1,0:T(8,128)S(1)}, f32[16,128]{1,0:T(8,128)S(1)}) all-reduce(f32[16,128]{1,0:T(8,128)S(1)} %stack.4, f32[16,128]{1,0:T(8,128)S(1)} %stack.5), channel_id=1, replica_groups=mesh['seq'=16,'ch'=2] {'seq','ch'}, use_global_device_ids=true, to_apply=%region_18.19 | all-reduce | flops 4096 | bytes 32768 | tf_op jit(solution)/shard_map/psum | solution.py:162
  (141 shorter events, 11.1 us)
Async XLA Ops:
  1.7 7.3 copy-start.13
  1.7 7.3 copy-start.15
  1.7 7.3 copy-start.17
  1.7 7.3 copy-start.19
  15.9 90.8 %all-to-all-start = ((f32[1,256,4224]{2,0,1:T(1,128)}), f32[1,256,4224]{2,0,1:T(1,128)}, u32[]{:S(2)}, u32[]{:S(2)}) async-start(f32[1,256,4224]{2,0,1:T(1,128)} %copy.44), calls=%async_computation | async-start | bytes 8650752 | tf_op jit(solution)/shard_map/all_to_all | solution.py:132
  137.9 180.1 %all-to-all-start.1 = ((f32[32,16,4224]{2,1,0:T(8,128)}), f32[32,16,4224]{2,1,0:T(8,128)}, u32[]{:S(2)}, u32[]{:S(2)}) async-start(f32[32,16,4224]{2,1,0:T(8,128)} %copy.47), calls=%async_computation.1 | async-start | bytes 17301504 | tf_op jit(solution)/shard_map/all_to_all | solution.py:136
  318.0 197.5 %all-to-all-start.2 = ((f32[32,16,4224]{2,1,0:T(8,128)}), f32[32,16,4224]{2,1,0:T(8,128)}, u32[]{:S(2)}, u32[]{:S(2)}) async-start(f32[32,16,4224]{2,1,0:T(8,128)} %copy.50), calls=%async_computation.2 | async-start | bytes 17301504 | tf_op jit(solution)/shard_map/all_to_all | solution.py:137
  519.6 38.9 %slice-start = ((s8[8650752]{0:T(1024)(128)(4,1)}), s8[4194304]{0:T(1024)(128)(4,1)S(1)}, s32[]{:S(2)}) async-start(s8[8650752]{0:T(1024)(128)(4,1)} %bitcast.367), calls=%async_computation.6 | async-start | bytes 8388608
  519.6 38.9 %slice-start.1 = ((s8[8650752]{0:T(1024)(128)(4,1)}), s8[4194304]{0:T(1024)(128)(4,1)S(1)}, s32[]{:S(2)}) async-start(s8[8650752]{0:T(1024)(128)(4,1)} %bitcast.367), calls=%async_computation.7 | async-start | bytes 8388608
  537.3 21.2 %slice-start.2 = ((s8[8650752]{0:T(1024)(128)(4,1)}), s8[262144]{0:T(1024)(128)(4,1)S(1)}, s32[]{:S(2)}) async-start(s8[8650752]{0:T(1024)(128)(4,1)} %bitcast.367), calls=%async_computation.8 | async-start | bytes 524288
  558.4 21.9 %slice-start.3 = ((s8[8650752]{0:T(1024)(128)(4,1)}), s8[4194304]{0:T(1024)(128)(4,1)S(1)}, s32[]{:S(2)}) async-start(s8[8650752]{0:T(1024)(128)(4,1)} %bitcast.374), calls=%async_computation.9 | async-start | bytes 8388608
  558.5 21.9 %slice-start.4 = ((s8[8650752]{0:T(1024)(128)(4,1)}), s8[4194304]{0:T(1024)(128)(4,1)S(1)}, s32[]{:S(2)}) async-start(s8[8650752]{0:T(1024)(128)(4,1)} %bitcast.374), calls=%async_computation.10 | async-start | bytes 8388608
  558.5 21.9 %slice-start.5 = ((s8[8650752]{0:T(1024)(128)(4,1)}), s8[262144]{0:T(1024)(128)(4,1)S(1)}, s32[]{:S(2)}) async-start(s8[8650752]{0:T(1024)(128)(4,1)} %bitcast.374), calls=%async_computation.11 | async-start | bytes 524288
  558.5 21.9 %slice-start.6 = ((f32[2,256,4224]{1,2,0:T(8,128)}), f32[2,256,128]{1,2,0:T(8,128)S(1)}, s32[]{:S(2)}) async-start(f32[2,256,4224]{1,2,0:T(8,128)} %add_bitcast_fusion.1), calls=%async_computation.12 | async-start | bytes 524288 | tf_op jit(solution)/shard_map/slice | solution.py:144
  596.3 13.4 %copy-start.1 = (f32[2,256,2048]{1,2,0:T(8,128)S(1)}, f32[2,256,2048]{1,2,0:T(8,128)}, u32[]{:S(2)}) copy-start(f32[2,256,2048]{1,2,0:T(8,128)} %get-tuple-element.60) | copy-start | bytes 12582916
  596.3 13.4 %copy-start.2 = (f32[2,256,2048]{1,2,0:T(8,128)S(1)}, f32[2,256,2048]{1,2,0:T(8,128)}, u32[]{:S(2)}) copy-start(f32[2,256,2048]{1,2,0:T(8,128)} %get-tuple-element.61) | copy-start | bytes 12582916
  609.7 13.3 %copy-start.3 = (f32[2,256,2048]{1,2,0:T(8,128)S(1)}, f32[2,256,2048]{1,2,0:T(8,128)}, u32[]{:S(2)}) copy-start(f32[2,256,2048]{1,2,0:T(8,128)} %get-tuple-element.59) | copy-start | bytes 12582916
  609.7 13.3 %copy-start.4 = (f32[2,256,2048]{1,2,0:T(8,128)S(1)}, f32[2,256,2048]{1,2,0:T(8,128)}, u32[]{:S(2)}) copy-start(f32[2,256,2048]{1,2,0:T(8,128)} %get-tuple-element.62) | copy-start | bytes 12582916
  670.8 196.5 %all-to-all-start.3 = ((f32[2,256,4224]{2,0,1:T(2,128)}), f32[2,256,4224]{2,0,1:T(2,128)}, u32[]{:S(2)}, u32[]{:S(2)}) async-start(f32[2,256,4224]{2,0,1:T(2,128)} %copy.55), calls=%async_computation.3 | async-start | bytes 17301504 | tf_op jit(solution)/shard_map/all_to_all | solution.py:153
  867.3 195.0 %all-to-all-start.4 = ((f32[2,256,4224]{2,0,1:T(2,128)}), f32[2,256,4224]{2,0,1:T(2,128)}, u32[]{:S(2)}, u32[]{:S(2)}) async-start(f32[2,256,4224]{2,0,1:T(2,128)} %copy.58), calls=%async_computation.4 | async-start | bytes 17301504 | tf_op jit(solution)/shard_map/all_to_all | solution.py:154
  1093.5 41.7 %copy-start.11 = (f32[16,128]{1,0:T(8,128)S(1)}, f32[16,128]{1,0:T(8,128)}, u32[]{:S(2)}) copy-start(f32[16,128]{1,0:T(8,128)} %get-tuple-element.165) | copy-start | bytes 24580
  1093.5 122.4 %copy-start.5 = (bf16[256,2048]{1,0:T(8,128)(2,1)S(1)}, bf16[256,2048]{1,0:T(8,128)(2,1)}, u32[]{:S(2)}) copy-start(bf16[256,2048]{1,0:T(8,128)(2,1)} %param.7) | copy-start | bytes 3145732
  1093.5 122.4 %copy-start.6 = (bf16[256,2048]{1,0:T(8,128)(2,1)S(1)}, bf16[256,2048]{1,0:T(8,128)(2,1)}, u32[]{:S(2)}) copy-start(bf16[256,2048]{1,0:T(8,128)(2,1)} %param.8) | copy-start | bytes 3145732
  1093.5 122.4 %copy-start.7 = (bf16[256,2048]{1,0:T(8,128)(2,1)S(1)}, bf16[256,2048]{1,0:T(8,128)(2,1)}, u32[]{:S(2)}) copy-start(bf16[256,2048]{1,0:T(8,128)(2,1)} %param.9) | copy-start | bytes 3145732
  1096.8 123.6 %copy-start.40 = (f32[128]{0:T(128)S(1)}, f32[128]{0:T(128)}, u32[]{:S(2)}) copy-start(f32[128]{0:T(128)} %copy-done.39) | copy-start | bytes 1540
  1096.8 123.6 %copy-start.42 = (f32[128]{0:T(128)S(1)}, f32[128]{0:T(128)}, u32[]{:S(2)}) copy-start(f32[128]{0:T(128)} %copy-done.41) | copy-start | bytes 1540
  1096.8 123.6 %copy-start.44 = (f32[128]{0:T(128)S(1)}, f32[128]{0:T(128)}, u32[]{:S(2)}) copy-start(f32[128]{0:T(128)} %copy-done.43) | copy-start | bytes 1540
  1096.8 123.6 %copy-start.45 = (f32[128]{0:T(128)S(1)}, f32[128]{0:T(128)}, u32[]{:S(2)}) copy-start(f32[128]{0:T(128)} %get-tuple-element.155) | copy-start | bytes 1540
  1096.8 123.6 %copy-start.46 = (f32[128]{0:T(128)S(1)}, f32[128]{0:T(128)}, u32[]{:S(2)}) copy-start(f32[128]{0:T(128)} %get-tuple-element.156) | copy-start | bytes 1540
  1096.9 123.6 %copy-start.47 = (f32[128]{0:T(128)S(1)}, f32[128]{0:T(128)}, u32[]{:S(2)}) copy-start(f32[128]{0:T(128)} %get-tuple-element.157) | copy-start | bytes 1540
  1096.9 123.6 %copy-start.49 = (f32[256]{0:T(256)S(1)}, f32[256]{0:T(256)}, u32[]{:S(2)}) copy-start(f32[256]{0:T(256)} %copy-done.48) | copy-start | bytes 3076
  1096.9 124.7 %copy-start.9 = (f32[16,128]{1,0:T(8,128)S(1)}, f32[16,128]{1,0:T(8,128)}, u32[]{:S(2)}) copy-start(f32[16,128]{1,0:T(8,128)} %copy-done.8) | copy-start | bytes 24580
  1096.9 124.7 %copy-start.34 = (f32[128]{0:T(128)S(1)}, f32[128]{0:T(128)}, u32[]{:S(2)}) copy-start(f32[128]{0:T(128)} %copy-done.33) | copy-start | bytes 1540
  1096.9 124.7 %copy-start.36 = (f32[128]{0:T(128)S(1)}, f32[128]{0:T(128)}, u32[]{:S(2)}) copy-start(f32[128]{0:T(128)} %copy-done.35) | copy-start | bytes 1540
  1096.9 124.7 %copy-start.38 = (f32[128]{0:T(128)S(1)}, f32[128]{0:T(128)}, u32[]{:S(2)}) copy-start(f32[128]{0:T(128)} %copy-done.37) | copy-start | bytes 1540
  1096.9 125.8 %copy-start.28 = (f32[128]{0:T(128)S(1)}, f32[128]{0:T(128)}, u32[]{:S(2)}) copy-start(f32[128]{0:T(128)} %copy-done.27) | copy-start | bytes 1540
  1096.9 125.8 %copy-start.30 = (f32[128]{0:T(128)S(1)}, f32[128]{0:T(128)}, u32[]{:S(2)}) copy-start(f32[128]{0:T(128)} %copy-done.29) | copy-start | bytes 1540
  1096.9 125.8 %copy-start.32 = (f32[128]{0:T(128)S(1)}, f32[128]{0:T(128)}, u32[]{:S(2)}) copy-start(f32[128]{0:T(128)} %copy-done.31) | copy-start | bytes 1540
  1096.9 126.9 %copy-start.22 = (f32[128]{0:T(128)S(1)}, f32[128]{0:T(128)}, u32[]{:S(2)}) copy-start(f32[128]{0:T(128)} %copy-done.21) | copy-start | bytes 1540
  1097.0 126.9 %copy-start.24 = (f32[128]{0:T(128)S(1)}, f32[128]{0:T(128)}, u32[]{:S(2)}) copy-start(f32[128]{0:T(128)} %copy-done.23) | copy-start | bytes 1540
  1097.0 126.9 %copy-start.26 = (f32[128]{0:T(128)S(1)}, f32[128]{0:T(128)}, u32[]{:S(2)}) copy-start(f32[128]{0:T(128)} %copy-done.25) | copy-start | bytes 1540
  1097.0 128.1 %copy-start.14 = (f32[128]{0:T(128)S(1)}, f32[128]{0:T(128)}, u32[]{:S(2)}) copy-start(f32[128]{0:T(128)} %copy-done.13) | copy-start | bytes 1540
  1097.0 128.1 %copy-start.16 = (f32[128]{0:T(128)S(1)}, f32[128]{0:T(128)}, u32[]{:S(2)}) copy-start(f32[128]{0:T(128)} %copy-done.15) | copy-start | bytes 1540
  1097.0 128.1 %copy-start.18 = (f32[128]{0:T(128)S(1)}, f32[128]{0:T(128)}, u32[]{:S(2)}) copy-start(f32[128]{0:T(128)} %copy-done.17) | copy-start | bytes 1540
  1097.0 128.1 %copy-start.20 = (f32[128]{0:T(128)S(1)}, f32[128]{0:T(128)}, u32[]{:S(2)}) copy-start(f32[128]{0:T(128)} %copy-done.19) | copy-start | bytes 1540
  1097.0 129.2 %copy-start.10 = (f32[16,128]{1,0:T(8,128)S(1)}, f32[16,128]{1,0:T(8,128)}, u32[]{:S(2)}) copy-start(f32[16,128]{1,0:T(8,128)} %param.11) | copy-start | bytes 24580
  1097.0 129.2 %copy-start.12 = (f32[16,128]{1,0:T(8,128)S(1)}, f32[16,128]{1,0:T(8,128)}, u32[]{:S(2)}) copy-start(f32[16,128]{1,0:T(8,128)} %param.10) | copy-start | bytes 24580
  1097.0 118.8 %all-to-all-start.5 = ((f32[16,16,4224]{2,1,0:T(8,128)}), f32[16,16,4224]{2,1,0:T(8,128)}, u32[]{:S(2)}, u32[]{:S(2)}) async-start(f32[16,16,4224]{2,1,0:T(8,128)} %copy.61), calls=%async_computation.5 | async-start | bytes 8650752 | tf_op jit(solution)/shard_map/all_to_all | solution.py:157
  (15 other events, 96.0 us)
where the time goes:
time: 1290 us; the launch traced here: 1280 us
  waiting for transfers between devices  708 us (55%)
  starting transfers between devices  187 us (14%)
  matrix products  175 us (14%)
  local copies, waits for them, and re-layouts  120 us (9%)
  blocking collectives  54.9 us (4%)
  other arithmetic  36 us (3%)
    dot_general x12, matrix products, contract(): return jnp.einsum(form, table, field, precision=highest)  175 us
    all_to_all x1, waiting for transfers between devices, shards(): lax.all_to_all(real_part, 'seq', split_axis=0, concat_axis=1, tiled=True)  148 us
    all_to_all x1, waiting for transfers between devices, shards(): lax.all_to_all(inner_re, 'seq', split_axis=1, concat_axis=0, tiled=True)  144 us
    all_to_all x1, waiting for transfers between devices, shards(): lax.all_to_all(imag_part, 'seq', split_axis=0, concat_axis=1, tiled=True)  131 us
    all_to_all x1, waiting for transfers between devices, shards(): lax.all_to_all(inner_im, 'seq', split_axis=1, concat_axis=0, tiled=True)  124 us
    all_to_all x1, waiting for transfers between devices, shards(): lax.all_to_all(stacked[None], 'seq', split_axis=1, concat_axis=0, tiled=T...  82 us
    all_to_all x1, waiting for transfers between devices, shards(): lax.all_to_all(time_re, 'seq', split_axis=0, concat_axis=1, tiled=True)  80.6 us
    psum x1, blocking collectives, shards(): firsts, seconds = lax.psum((firsts, seconds), ('seq', 'ch'))  54.9 us
  transfers between devices with their start and end apart: 6, of which 6 were waited for; matrix products, arithmetic and copies ran while one was open for 5% of the time, Pallas kernels for 0%

commit v1 on v0

v1 whole, which is shorter than its diff:
```python
import functools
import math

import jax
import jax.numpy as jnp
from jax import lax
from jax.experimental import pallas as pl
from jax.experimental.pallas import tpu as pltpu
from jax.sharding import PartitionSpec as P

SUBS = 8
LANES = 128
TILE = 4


def wide(row):
    return jnp.broadcast_to(row, (SUBS, LANES))


def fill_impulse(imp_ref, wgt_ref, dec_ref, length):
    modes = dec_ref.shape[0]
    lag = lax.broadcasted_iota(jnp.int32, (SUBS, LANES), 0)
    for block in range(length // SUBS):
        lags = (lag + block * SUBS).astype(jnp.float32)
        total = jnp.zeros((SUBS, LANES), jnp.float32)
        for m in range(modes):
            rate = dec_ref[m : m + 1, :]
            weight = wgt_ref[m : m + 1, :]
            total = total + weight * jnp.exp(-rate * lags)
        for i in range(SUBS):
            imp_ref[block * SUBS + i] = wide(total[i : i + 1, :])


def split_tokens(nat_ref, out_ref, length):
    for j in range(length):
        out_ref[j] = nat_ref[pl.ds(j, SUBS, stride=length), :]


def join_tokens(nat_ref, pieces, length):
    for j in range(length):
        nat_ref[pl.ds(j, SUBS, stride=length), :] = pieces[j]


def near_lags(u_ref, s_ref, imp_ref, conv, back, corr, length):
    tiles = length // TILE
    for j in range(length):
        conv[j] = jnp.zeros((SUBS, LANES), jnp.float32)
        back[j] = jnp.zeros((SUBS, LANES), jnp.float32)
    for delta in range(tiles):
        lags = [d for d in range(TILE * delta - TILE + 1, TILE * delta + TILE) if d >= 0]
        imp = {d: imp_ref[d] for d in lags}
        sums = {d: corr[d] for d in lags}
        for first in range(tiles - delta):
            sources = range(TILE * first, TILE * first + TILE)
            targets = range(TILE * (first + delta), TILE * (first + delta) + TILE)
            us = {s: u_ref[s] for s in sources}
            ss = {t: s_ref[t] for t in targets}
            cs = {t: conv[t] for t in targets}
            bs = {s: back[s] for s in sources}
            for t in targets:
                for s in sources:
                    if t >= s:
                        cs[t] = cs[t] + imp[t - s] * us[s]
                        bs[s] = bs[s] + imp[t - s] * ss[t]
                        sums[t - s] = sums[t - s] + us[s] * ss[t]
            for t in targets:
                conv[t] = cs[t]
            for s in sources:
                back[s] = bs[s]
        for d in lags:
            corr[d] = sums[d]


def block_states(u_ref, s_ref, dec_ref, modes, length):
    zero = jnp.zeros((SUBS, LANES), jnp.float32)
    decay = [wide(jnp.exp(-dec_ref[m : m + 1, :])) for m in modes]
    hs = [zero for _ in modes]
    h1s = [zero for _ in modes]
    gs = [zero for _ in modes]
    g1s = [zero for _ in modes]
    for j in range(length):
        u = u_ref[j]
        s = s_ref[length - 1 - j]
        for n in range(len(decay)):
            moved = decay[n] * hs[n]
            h1s[n] = decay[n] * h1s[n] + moved
            hs[n] = moved + u
            moved = decay[n] * gs[n]
            g1s[n] = decay[n] * g1s[n] + moved
            gs[n] = moved + s
    out = []
    for n in range(len(decay)):
        moved = decay[n] * hs[n]
        out.append((moved, decay[n] * h1s[n] + moved, gs[n], g1s[n]))
    return out


def local_kernel(
    length, k_ref, v_ref, g_ref, q_ref, wgt_ref, dec_ref,
    conv_ref, back_ref, hin_ref, gin_ref, state_ref, slope_ref, sums_ref,
    nat_ref, u_ref, s_ref, imp_ref, corr_ref, first_ref, second_ref,
):
    group = pl.program_id(0)
    modes = dec_ref.shape[0]

    @pl.when(group == 0)
    def _():
        fill_impulse(imp_ref, wgt_ref, dec_ref, length)
        corr_ref[...] = jnp.zeros_like(corr_ref)
        first_ref[...] = jnp.zeros_like(first_ref)
        second_ref[...] = jnp.zeros_like(second_ref)

    nat_ref[...] = k_ref[...].astype(jnp.float32) * v_ref[...].astype(jnp.float32)
    split_tokens(nat_ref, u_ref, length)
    nat_ref[...] = g_ref[...].astype(jnp.float32) * q_ref[...].astype(jnp.float32)
    split_tokens(nat_ref, s_ref, length)

    sub = lax.broadcasted_iota(jnp.int32, (SUBS, LANES), 0)
    half = modes // 2
    for start in range(0, modes, half):
        ids = range(start, start + half)
        for m, (h, h1, g, g1) in zip(ids, block_states(u_ref, s_ref, dec_ref, ids, length)):
            rate = wide(dec_ref[m : m + 1, :])
            ih, ih1, ig, ig1 = h, h1, g, g1
            step = 1
            while step < SUBS:
                span = float(step * length)
                power = jnp.exp(-span * rate)
                up = jnp.where(sub >= step, power, 0.0)
                down = jnp.where(sub < SUBS - step, power, 0.0)
                rh = pltpu.roll(ih, step, 0)
                rh1 = pltpu.roll(ih1, step, 0)
                ih1 = ih1 + up * (rh1 + span * rh)
                ih = ih + up * rh
                rg = pltpu.roll(ig, SUBS - step, 0)
                rg1 = pltpu.roll(ig1, SUBS - step, 0)
                ig1 = ig1 + down * (rg1 + span * rg)
                ig = ig + down * rg
                step *= 2
            hin = jnp.where(sub >= 1, pltpu.roll(ih, 1, 0), 0.0)
            h1in = jnp.where(sub >= 1, pltpu.roll(ih1, 1, 0), 0.0)
            gin = jnp.where(sub < SUBS - 1, pltpu.roll(ig, SUBS - 1, 0), 0.0)
            hin_ref[0, m] = hin
            gin_ref[0, m] = gin
            state_ref[0, 0, m : m + 1, :] = ih[SUBS - 1 :, :]
            state_ref[0, 1, m : m + 1, :] = ig[:1, :]
            slope_ref[0, 0, m : m + 1, :] = ih1[SUBS - 1 :, :]
            slope_ref[0, 1, m : m + 1, :] = ig1[:1, :]
            first_ref[m] += g * hin
            second_ref[m] += g1 * hin + g * h1in

    near_lags(u_ref, s_ref, imp_ref, conv_ref.at[0], back_ref.at[0], corr_ref, length)

    @pl.when(group == pl.num_programs(0) - 1)
    def _():
        corr = [jnp.sum(corr_ref[j], axis=0, keepdims=True) for j in range(length)]
        packs = [jnp.concatenate(corr[b : b + SUBS], axis=0) for b in range(0, length, SUBS)]
        for m in range(modes):
            rate = dec_ref[m : m + 1, :]
            first = first_ref[m]
            second = second_ref[m]
            for b in range(len(packs)):
                lags = (sub + b * SUBS).astype(jnp.float32)
                term = packs[b] * jnp.exp(-rate * lags)
                first = first + term
                second = second + term * lags
            sums_ref[0, m : m + 1, :] = jnp.sum(first, axis=0, keepdims=True)
            sums_ref[1, m : m + 1, :] = jnp.sum(second, axis=0, keepdims=True)


def local_pass(query, key_in, values, cotangent, weights, decay_rates):
    rows, channels = query.shape
    modes, filters = decay_rates.shape
    groups = channels // filters
    length = rows // SUBS
    column = pl.BlockSpec((rows, filters), lambda g: (0, g))
    small = pl.BlockSpec((modes, filters), lambda g: (0, 0))
    f32 = jnp.float32
    piece = pl.BlockSpec((1, length, SUBS, filters), lambda g: (g, 0, 0, 0))
    inner = pl.BlockSpec((1, modes, SUBS, filters), lambda g: (g, 0, 0, 0))
    pair = pl.BlockSpec((1, 2, modes, filters), lambda g: (g, 0, 0, 0))
    return pl.pallas_call(
        functools.partial(local_kernel, length),
        grid=(groups,),
        in_specs=[column] * 4 + [small] * 2,
        out_specs=[piece, piece, inner, inner, pair, pair,
                   pl.BlockSpec((2, modes, filters), lambda g: (0, 0, 0))],
        out_shape=[
            jax.ShapeDtypeStruct((groups, length, SUBS, filters), f32),
            jax.ShapeDtypeStruct((groups, length, SUBS, filters), f32),
            jax.ShapeDtypeStruct((groups, modes, SUBS, filters), f32),
            jax.ShapeDtypeStruct((groups, modes, SUBS, filters), f32),
            jax.ShapeDtypeStruct((groups, 2, modes, filters), f32),
            jax.ShapeDtypeStruct((groups, 2, modes, filters), f32),
            jax.ShapeDtypeStruct((2, modes, filters), f32),
        ],
        scratch_shapes=[
            pltpu.VMEM((rows, filters), f32),
            pltpu.VMEM((length, SUBS, filters), f32),
            pltpu.VMEM((length, SUBS, filters), f32),
            pltpu.VMEM((length, SUBS, filters), f32),
            pltpu.VMEM((length, SUBS, filters), f32),
            pltpu.VMEM((modes, SUBS, filters), f32),
            pltpu.VMEM((modes, SUBS, filters), f32),
        ],
        compiler_params=pltpu.CompilerParams(vmem_limit_bytes=32 * 1024 * 1024),
        name="local_pass",
    )(key_in, values, cotangent, query, weights, decay_rates)


def owner_kernel(span, x_ref, dec_ref, y_ref, first_ref, second_ref):
    devices = x_ref.shape[0]
    power = jnp.exp(-span * dec_ref[...])
    state = jnp.zeros_like(dec_ref[...])
    slope = state
    first = state
    second = state
    for d in range(devices):
        y_ref[d, 0] = state
        first = first + x_ref[d, 1] * state
        second = second + x_ref[d, 1] * slope
        slope = power * (slope + span * state)
        state = power * state + x_ref[d, 0]
    state = jnp.zeros_like(dec_ref[...])
    for d in reversed(range(devices)):
        y_ref[d, 1] = state
        state = power * state + x_ref[d, 1]
    first_ref[...] = first
    second_ref[...] = second


def owner_pass(received, rates, span):
    f32 = jnp.float32
    return pl.pallas_call(
        functools.partial(owner_kernel, span),
        out_shape=[
            jax.ShapeDtypeStruct(received.shape, f32),
            jax.ShapeDtypeStruct(rates.shape, f32),
            jax.ShapeDtypeStruct(rates.shape, f32),
        ],
        name="owner_pass",
    )(received, rates)


def finish_kernel(
    length, k_ref, v_ref, g_ref, wgt_ref, dec_ref, conv_ref, back_ref, hin_ref, gin_ref, far_ref,
    dq_ref, dk_ref, dv_ref, nat_ref,
):
    modes = dec_ref.shape[0]
    sub = lax.broadcasted_iota(jnp.int32, (SUBS, LANES), 0).astype(jnp.float32)
    decay = []
    ahead = []
    behind = []
    for m in range(modes):
        rate = dec_ref[m : m + 1, :]
        weight = wgt_ref[m : m + 1, :]
        decay.append(wide(jnp.exp(-rate)))
        before = jnp.exp(-rate * (sub * float(length)))
        after = jnp.exp(-rate * ((SUBS - 1.0 - sub) * float(length)))
        ahead.append(weight * (hin_ref[0, m] + before * far_ref[0, 0, m : m + 1, :]))
        behind.append(weight * (gin_ref[0, m] + after * far_ref[0, 1, m : m + 1, :]))

    def total(parts):
        while len(parts) > 1:
            parts = [sum(parts[i : i + 2]) for i in range(0, len(parts), 2)]
        return parts[0]

    for j in range(length):
        nat_ref[pl.ds(j, SUBS, stride=length), :] = conv_ref[0, j] + total(ahead)
        ahead = [x * a for x, a in zip(ahead, decay)]
    dq_ref[...] = (g_ref[...].astype(jnp.float32) * nat_ref[...]).astype(jnp.bfloat16)
    for j in reversed(range(length)):
        behind = [x * a for x, a in zip(behind, decay)]
        nat_ref[pl.ds(j, SUBS, stride=length), :] = back_ref[0, j] + total(behind)
    dk_ref[...] = (v_ref[...].astype(jnp.float32) * nat_ref[...]).astype(jnp.bfloat16)
    dv_ref[...] = (k_ref[...].astype(jnp.float32) * nat_ref[...]).astype(jnp.bfloat16)


def finish_pass(key_in, values, cotangent, weights, decay_rates, conv, back, hin, gin, far):
    rows, channels = key_in.shape
    modes, filters = decay_rates.shape
    groups = channels // filters
    length = rows // SUBS
    column = pl.BlockSpec((rows, filters), lambda g: (0, g))
    small = pl.BlockSpec((modes, filters), lambda g: (0, 0))
    piece = pl.BlockSpec((1, length, SUBS, filters), lambda g: (g, 0, 0, 0))
    inner = pl.BlockSpec((1, modes, SUBS, filters), lambda g: (g, 0, 0, 0))
    pair = pl.BlockSpec((1, 2, modes, filters), lambda g: (g, 0, 0, 0))
    return pl.pallas_call(
        functools.partial(finish_kernel, length),
        grid=(groups,),
        in_specs=[column] * 3 + [small] * 2 + [piece, piece, inner, inner, pair],
        out_specs=[column] * 3,
        out_shape=[jax.ShapeDtypeStruct((rows, channels), jnp.bfloat16)] * 3,
        scratch_shapes=[pltpu.VMEM((rows, filters), jnp.float32)],
        compiler_params=pltpu.CompilerParams(vmem_limit_bytes=32 * 1024 * 1024),
        name="finish_pass",
    )(key_in, values, cotangent, weights, decay_rates, conv, back, hin, gin, far)


def shards(query, key_in, values, cotangent, residues, decay_rates):
    devices = lax.axis_size("seq")
    me = lax.axis_index("seq")
    rows, channels = query.shape
    modes, filters = decay_rates.shape
    groups = channels // filters
    share = groups * modes // devices
    scale = jnp.sqrt(-jnp.expm1(-2.0 * decay_rates))
    weights = residues * scale
    conv, back, hin, gin, states, slopes, sums = local_pass(
        query, key_in, values, cotangent, weights, decay_rates
    )
    sent = states.transpose(0, 2, 1, 3).reshape(devices, share, 2, filters).transpose(0, 2, 1, 3)
    received = lax.all_to_all(sent, "seq", split_axis=0, concat_axis=0, tiled=True)
    row_rates = jnp.tile(decay_rates, (groups, 1)).reshape(devices, share, filters)
    own_rates = lax.dynamic_index_in_dim(row_rates, me, 0, keepdims=False)
    answer, first, second = owner_pass(received, own_rates, float(rows))
    far = lax.all_to_all(answer, "seq", split_axis=0, concat_axis=0, tiled=True)
    far = far.transpose(0, 2, 1, 3).reshape(groups, modes, 2, filters).transpose(0, 2, 1, 3)
    crossing = jnp.sum(slopes[:, 1] * far[:, 0] + slopes[:, 0] * far[:, 1], axis=0)
    owned = jnp.zeros((2, groups * modes, filters), jnp.float32)
    owned = lax.dynamic_update_slice(owned, jnp.stack([first, second]), (0, me * share, 0))
    owned = owned.reshape(2, groups, modes, filters).sum(1)
    zeroth = sums[0] + owned[0]
    moment = sums[1] + owned[1] + crossing
    zeroth, moment = lax.psum((zeroth, moment), ("seq", "ch"))
    query_grad, key_grad, value_grad = finish_pass(
        key_in, values, cotangent, weights, decay_rates, conv, back, hin, gin, far
    )
    norm_factor = 1.0 / math.sqrt(devices * rows)
    slope = jnp.exp(-2.0 * decay_rates) / scale
    residue_grad = scale * zeroth * norm_factor
    rate_grad = decay_rates * residues * (slope * zeroth - scale * moment) * norm_factor
    return (query_grad, key_grad, value_grad, residue_grad, rate_grad)


def solution(mesh):
    in_specs = (P("seq", "ch"), P("seq", "ch"), P("seq", "ch"), P("seq", "ch"), P(), P())
    out_specs = (P("seq", "ch"), P("seq", "ch"), P("seq", "ch"), P(), P())
    return jax.shard_map(shards, mesh=mesh, in_specs=in_specs, out_specs=out_specs, check_vma=False)
```

time: 1290 us -> 125 us (0.10)
  waiting for transfers between devices: 708 us -> 6.19 us
  starting transfers between devices: 187 us -> 3.55 us
  matrix products: 175 us -> 0 us
  local copies, waits for them, and re-layouts: 120 us -> 17.2 us
  Pallas kernels: 0 us -> 34.2 us
  other arithmetic: 36 us -> 4.67 us
    all_to_all x6 -> x1, waiting for transfers between devices: 708 us -> 6.19 us  [shards(): far = lax.all_to_all(answer, 'seq', split_axis=0, concat_axis=0, tiled=True)]
    all_to_all x6 -> x1, starting transfers between devices: 187 us -> 3.55 us  [shards(): far = lax.all_to_all(answer, 'seq', split_axis=0, concat_axis=0, tiled=True)]
    dot_general x12 -> x0, matrix products: 175 us -> none  [contract(): return jnp.einsum(form, table, field, precision=highest)]
    all_to_all x8 -> x0, local copies, waits for them, and re-layouts: 54.9 us -> none  [the longest x3 23.4 us: shards(): lax.all_to_all(inner_im, 'seq', split_axis=1, concat_axis=0, tiled=True)]
    pallas_call x0 -> x3, Pallas kernels: none -> 34.2 us  [the longest x1 23.1 us: local_pass(): pl.pallas_call(functools.partial(local_kernel, length), grid=(groups,), i...]
    sub x3 -> x0, local copies, waits for them, and re-layouts: 25.7 us -> none  [the longest x1 14 us: row_inverse(): new_real * cos_twist - new_imag * sin_twist]
    add x2 -> x0, local copies, waits for them, and re-layouts: 22.3 us -> none  [the longest x1 13.9 us: row_inverse(): new_imag * cos_twist + new_real * sin_twist]
    all_to_all x0 -> x1, blocking collectives: none -> 18.2 us  [shards(): lax.all_to_all(sent, 'seq', split_axis=0, concat_axis=0, tiled=True)]
  transfers between devices with their start and end apart: 6 -> 1, of which waited for: 6 -> 1; matrix products, arithmetic and copies ran while one was open for 5% -> 2% of each run, Pallas kernels for 0% -> 0%
where the time goes in v1:
time: 125 us; the launch traced here: 124 us
  blocking collectives  57.2 us (46%)
  Pallas kernels  34.2 us (27%)
  local copies, waits for them, and re-layouts  17.2 us (14%)
  waiting for transfers between devices  6.19 us (5%)
  other arithmetic  4.67 us (4%)
  starting transfers between devices  3.55 us (3%)
    psum x1, blocking collectives, shards(): zeroth, moment = lax.psum((zeroth, moment), ('seq', 'ch'))  39 us
    pallas_call x1, Pallas kernels, local_pass(): pl.pallas_call(functools.partial(local_kernel, length), grid=(groups,), i...  23.1 us
    all_to_all x1, blocking collectives, shards(): lax.all_to_all(sent, 'seq', split_axis=0, concat_axis=0, tiled=True)  18.2 us
    unnamed x38, local copies, waits for them, and re-layouts  16.5 us
    pallas_call x1, Pallas kernels, finish_pass(): pl.pallas_call(functools.partial(finish_kernel, length), grid=(groups,),...  9.33 us
    all_to_all x1, waiting for transfers between devices, shards(): far = lax.all_to_all(answer, 'seq', split_axis=0, concat_axis=0, tiled=True)  6.19 us
    all_to_all x1, starting transfers between devices, shards(): far = lax.all_to_all(answer, 'seq', split_axis=0, concat_axis=0, tiled=True)  3.55 us
  transfers between devices with their start and end apart: 1, of which 1 were waited for; matrix products, arithmetic and copies ran while one was open for 2% of the time, Pallas kernels for 0%

profile of v1, /device:TPU:0, one launch (start us, length us, event | category | flops | bytes accessed | tf_op | source)
XLA Modules:
  0.0 123.8 jit_solution(1103513047887721453)
XLA Ops:
  0.6 0.7 fusion.5.wgt_ref
  1.4 0.0 copy-start
  1.4 1.2 copy-done
  2.6 0.0 copy-start.2
  2.6 1.2 copy-done.2
  3.8 0.0 copy-start.4
  3.8 1.2 copy-done.4
  5.0 1.2 copy-done.14
  6.3 0.0 copy-start.16
  6.3 0.7 copy-done.16
  7.0 0.0 copy-start.5
  7.0 23.1 %local_pass.1 = (f32[16,32,8,128]{3,2,1,0:T(8,128)S(1)}, f32[16,32,8,128]{3,2,1,0:T(8,128)S(1)}, f32[16,16,8,128]{3,2,1,0:T(8,128)S(1)}, f32[16,16,8,128]{3,2,1,...) custom-call(bf16[256,2048]{1,0:T(8,128)(2,1)S(1)} %copy-done, ...), custom_call_target="tpu_custom_call" | custom-call | tf_op jit(solution)/shard_map/local_pass/pallas_call | solution.py:182
  30.1 0.0 copy-start.6
  30.1 1.3 %copy-done.6 = f32[16,32,8,128]{3,2,1,0:T(8,128)} copy-done((f32[16,32,8,128]{3,2,1,0:T(8,128)}, f32[16,32,8,128]{3,2,1,0:T(8,128)S(1)}, u32[]{:S(2)}) %copy-start.6) | copy-done | bytes 2097176
  31.5 0.0 copy-start.8
  31.5 1.3 %copy-done.8 = f32[16,32,8,128]{3,2,1,0:T(8,128)} copy-done((f32[16,32,8,128]{3,2,1,0:T(8,128)}, f32[16,32,8,128]{3,2,1,0:T(8,128)S(1)}, u32[]{:S(2)}) %copy-start.8) | copy-done | bytes 2097176
  32.8 0.0 copy-start.10
  32.8 1.0 copy-done.10
  33.8 0.0 copy-start.12
  33.8 1.0 copy-done.12
  34.7 0.0 copy-start.15
  34.7 0.7 copy-done.15
  35.4 0.0 copy-start.18
  35.4 0.0 copy-start.1
  35.4 0.0 copy-start.3
  35.4 18.2 %all_to_all.10.x_ref = f32[16,2,16,128]{3,2,1,0:T(8,128)} all-to-all(f32[16,2,16,128]{3,2,1,0:T(8,128)S(1)} %get-tuple-element.22), channel_id=1, replica_groups=mesh['seq'=16,'ch'=2] {'seq'}, dimensions={0} | all-to-all | bytes 524288 | tf_op jit(solution)/shard_map/all_to_all | solution.py:314
  53.7 1.7 %owner_pass.1 = (f32[16,2,16,128]{3,2,1,0:T(8,128)}, f32[16,128]{1,0:T(8,128)}, f32[16,128]{1,0:T(8,128)}) custom-call(f32[16,2,16,128]{3,2,1,0:T(8,128)} %all_to_all.10.x_ref, f32[16,128]{1,0:T(8,128)} %dec_ref.4), custom_call_target="tpu_custom_call" | custom-call | tf_op jit(solution)/shard_map/owner_pass/pallas_call | solution.py:234
  55.4 3.5 %all-to-all-start.1 = ((f32[16,2,16,128]{3,2,1,0:T(8,128)}), f32[16,2,16,128]{3,2,1,0:T(8,128)S(1)}, u32[]{:S(2)}, u32[]{:S(2)}) async-start(f32[16,2,16,128]{3,2,1,0:T(8,128)} %get-tuple-element.23), calls=%async_computation.1 | async-start | bytes 524288 | tf_op jit(solution)/shard_map/all_to_all | solution.py:318
  58.9 0.7 broadcast_in_dim.3
  59.6 1.3 %maximum_dynamic-update-slice_fusion = f32[2,256,128]{2,1,0:T(8,128)} fusion(f32[2,256,128]{2,1,0:T(8,128)} %broadcast_in_dim.3, s32[]{:T(128)S(6)} %select_n.5, f32[1,16,128]{2,1,0:T(8,128)} %bitcast.10, f32[1,16,128]{2,1,0:T(8,128)} %bitcast.9), kind=kLoop, calls=%fused_computation.4 | loop fusion | flops 4096 | bytes 32772 | tf_op jit(solution)/shard_map/dynamic_update_slice | solution.py:322
  61.0 1.0 reduce_sum.18
  61.9 6.2 %all-to-all-done.1.far_ref = f32[16,2,16,128]{3,2,1,0:T(8,128)S(1)} async-done(((f32[16,2,16,128]{3,2,1,0:T(8,128)}), f32[16,2,16,128]{3,2,1,0:T(8,128)S(1)}, u32[]{:S(2)}, u32[]{:S(2)}) %all-to-all-start.1) | async-done | bytes 262176 | tf_op jit(solution)/shard_map/all_to_all | solution.py:318
  68.1 1.0 fusion.1
  69.2 39.0 %all-reduce = (f32[16,128]{1,0:T(8,128)S(1)}, f32[16,128]{1,0:T(8,128)S(1)}) all-reduce(f32[16,128]{1,0:T(8,128)S(1)} %fusion.4, f32[16,128]{1,0:T(8,128)S(1)} %fusion.3), channel_id=1, replica_groups=mesh['seq'=16,'ch'=2] {'seq','ch'}, use_global_device_ids=true, to_apply=%region_1.2 | all-reduce | flops 4096 | bytes 32768 | tf_op jit(solution)/shard_map/psum | solution.py:326
  108.1 0.0 copy-done.17
  108.1 0.0 copy-done.18
  108.2 0.6 multiply_multiply_fusion
  108.8 0.0 copy-done.5
  108.8 0.0 copy-done.1
  108.8 0.0 copy-done.3
  108.8 0.0 copy-start.7
  108.8 1.6 %copy-done.7 = f32[16,32,8,128]{3,2,1,0:T(8,128)S(1)} copy-done((f32[16,32,8,128]{3,2,1,0:T(8,128)S(1)}, f32[16,32,8,128]{3,2,1,0:T(8,128)}, u32[]{:S(2)}) %copy-start.7) | copy-done | bytes 2097176
  110.4 0.0 copy-start.9
  110.4 1.6 %copy-done.9 = f32[16,32,8,128]{3,2,1,0:T(8,128)S(1)} copy-done((f32[16,32,8,128]{3,2,1,0:T(8,128)S(1)}, f32[16,32,8,128]{3,2,1,0:T(8,128)}, u32[]{:S(2)}) %copy-start.9) | copy-done | bytes 2097176
  112.0 0.0 copy-start.11
  112.0 1.2 copy-done.11
  113.2 1.2 copy-done.13
  114.4 9.3 %finish_pass.1 = (bf16[256,2048]{1,0:T(8,128)(2,1)}, bf16[256,2048]{1,0:T(8,128)(2,1)}, bf16[256,2048]{1,0:T(8,128)(2,1)}) custom-call(bf16[256,2048]{1,0:T(8,128)(2,1)S(1)} %copy-done.1, bf16[256,2048]{1,0:T(8,128)(2,1)S(1)} %copy-done.3, bf16[256,2048]{1,0:T(8,128)(2,1)S(1)} %copy-done.5, f32[16,128]{1,0:T(8,128)S(1)} %fusion.5.wgt_ref, ...), custom_call_target="tpu_custom_call" | custom-call | tf_op jit(solution)/shard_map/finish_pass/pallas_call | solution.py:289
  (5 shorter events, 0.0 us)
Async XLA Ops:
  1.4 1.2 copy-start
  2.6 1.2 copy-start.2
  3.8 1.2 copy-start.4
  5.0 1.2 copy-start.14
  6.3 0.7 copy-start.16
  7.0 101.8 %copy-start.5 = (bf16[256,2048]{1,0:T(8,128)(2,1)S(1)}, bf16[256,2048]{1,0:T(8,128)(2,1)}, u32[]{:S(2)}) copy-start(bf16[256,2048]{1,0:T(8,128)(2,1)} %g_ref.3) | copy-start | bytes 3145732
  30.1 1.3 %copy-start.6 = (f32[16,32,8,128]{3,2,1,0:T(8,128)}, f32[16,32,8,128]{3,2,1,0:T(8,128)S(1)}, u32[]{:S(2)}) copy-start(f32[16,32,8,128]{3,2,1,0:T(8,128)S(1)} %get-tuple-element.18.conv_ref) | copy-start | bytes 6291460
  31.5 1.3 %copy-start.8 = (f32[16,32,8,128]{3,2,1,0:T(8,128)}, f32[16,32,8,128]{3,2,1,0:T(8,128)S(1)}, u32[]{:S(2)}) copy-start(f32[16,32,8,128]{3,2,1,0:T(8,128)S(1)} %get-tuple-element.19.back_ref) | copy-start | bytes 6291460
  32.8 1.0 copy-start.10
  33.8 1.0 copy-start.12
  34.7 0.7 copy-start.15
  35.4 72.7 %copy-start.17 = (f32[16,128]{1,0:T(8,128)S(1)}, f32[16,128]{1,0:T(8,128)}, u32[]{:S(2)}) copy-start(f32[16,128]{1,0:T(8,128)} %dec_ref.4) | copy-start | bytes 24580
  35.4 72.7 %copy-start.18 = (f32[16,128]{1,0:T(8,128)S(1)}, f32[16,128]{1,0:T(8,128)}, u32[]{:S(2)}) copy-start(f32[16,128]{1,0:T(8,128)} %param.10) | copy-start | bytes 24580
  35.4 73.3 %copy-start.1 = (bf16[256,2048]{1,0:T(8,128)(2,1)S(1)}, bf16[256,2048]{1,0:T(8,128)(2,1)}, u32[]{:S(2)}) copy-start(bf16[256,2048]{1,0:T(8,128)(2,1)} %k_ref.3) | copy-start | bytes 3145732
  35.4 73.3 %copy-start.3 = (bf16[256,2048]{1,0:T(8,128)(2,1)S(1)}, bf16[256,2048]{1,0:T(8,128)(2,1)}, u32[]{:S(2)}) copy-start(bf16[256,2048]{1,0:T(8,128)(2,1)} %v_ref.3) | copy-start | bytes 3145732
  55.4 12.8 %all-to-all-start.1 = ((f32[16,2,16,128]{3,2,1,0:T(8,128)}), f32[16,2,16,128]{3,2,1,0:T(8,128)S(1)}, u32[]{:S(2)}, u32[]{:S(2)}) async-start(f32[16,2,16,128]{3,2,1,0:T(8,128)} %get-tuple-element.23), calls=%async_computation.1 | async-start | bytes 524288 | tf_op jit(solution)/shard_map/all_to_all | solution.py:318
  108.8 1.6 %copy-start.7 = (f32[16,32,8,128]{3,2,1,0:T(8,128)S(1)}, f32[16,32,8,128]{3,2,1,0:T(8,128)}, u32[]{:S(2)}) copy-start(f32[16,32,8,128]{3,2,1,0:T(8,128)} %copy-done.6) | copy-start | bytes 6291460
  110.4 1.6 %copy-start.9 = (f32[16,32,8,128]{3,2,1,0:T(8,128)S(1)}, f32[16,32,8,128]{3,2,1,0:T(8,128)}, u32[]{:S(2)}) copy-start(f32[16,32,8,128]{3,2,1,0:T(8,128)} %copy-done.8) | copy-start | bytes 6291460
  112.0 1.2 copy-start.11
  113.2 1.2 copy-start.13

commit v2 on v1

--- a/solution.py
+++ b/solution.py
@@ -203,7 +203,7 @@
             pltpu.VMEM((modes, SUBS, filters), f32),
             pltpu.VMEM((modes, SUBS, filters), f32),
         ],
-        compiler_params=pltpu.CompilerParams(vmem_limit_bytes=32 * 1024 * 1024),
+        compiler_params=pltpu.CompilerParams(vmem_limit_bytes=60 * 1024 * 1024),
         name="local_pass",
     )(key_in, values, cotangent, query, weights, decay_rates)
 
@@ -242,6 +242,177 @@
     )(received, rates)
 
 
+def exchange_kernel(
+    span, x_ref, slope_ref, sums_ref, dec_ref, far_ref, total_ref,
+    got, ans, back, part, red, mine, gath,
+    send1, recv1, send2, recv2, send3, recv3, send4, recv4,
+):
+    devices = x_ref.shape[0]
+    cores = gath.shape[0] // devices
+    everyone = devices * cores
+    me = lax.axis_index("seq")
+    ch = lax.axis_index("ch")
+    my = ch * devices + me
+    mesh_ids = pl.DeviceIdType.MESH
+
+    def seq_copy(source, target, sends, recvs, peer, slot):
+        return pltpu.make_async_remote_copy(
+            src_ref=source.at[peer], dst_ref=target.at[slot], send_sem=sends.at[peer],
+            recv_sem=recvs.at[slot], device_id=(peer, ch), device_id_type=mesh_ids,
+        )
+
+    def swap_start(source, target, sends, recvs):
+        def body(step, carry):
+            peer = lax.rem(me + step, devices)
+            seq_copy(source, target, sends, recvs, peer, me).start()
+            return carry
+
+        lax.fori_loop(1, devices, body, 0)
+
+    def swap_wait(source, target, sends, recvs):
+        def body(step, carry):
+            peer = lax.rem(me + step, devices)
+            seq_copy(source, target, sends, recvs, peer, peer).wait()
+            return carry
+
+        lax.fori_loop(1, devices, body, 0)
+
+    barrier = pltpu.get_barrier_semaphore()
+
+    def greet(step, carry):
+        other = lax.rem(my + step, everyone)
+        pl.semaphore_signal(
+            barrier, inc=1, device_id=(lax.rem(other, devices), other // devices),
+            device_id_type=mesh_ids,
+        )
+        return carry
+
+    lax.fori_loop(1, everyone, greet, 0)
+    pl.semaphore_wait(barrier, everyone - 1)
+
+    swap_start(x_ref, got, send1, recv1)
+    got[me] = x_ref[me]
+    power = jnp.exp(-span * dec_ref[...])
+    swap_wait(x_ref, got, send1, recv1)
+    zero = jnp.zeros_like(power)
+    state, slope, first, second = zero, zero, zero, zero
+    for d in range(devices):
+        ans[d, 0] = state
+        first = first + got[d, 1] * state
+        second = second + got[d, 1] * slope
+        slope = power * (slope + span * state)
+        state = power * state + got[d, 0]
+    state = zero
+    for d in reversed(range(devices)):
+        ans[d, 1] = state
+        state = power * state + got[d, 1]
+
+    swap_start(ans, back, send2, recv2)
+    back[me] = ans[me]
+    swap_wait(ans, back, send2, recv2)
+    first = first + sums_ref[0]
+    second = second + sums_ref[1]
+    for d in range(devices):
+        second = second + slope_ref[d, 1] * back[d, 0] + slope_ref[d, 0] * back[d, 1]
+        far_ref[d] = back[d]
+
+    rows = part.shape[1]
+    half = devices // 2
+    for d in range(half):
+        part[d] = first[d * rows : (d + 1) * rows, :]
+        part[half + d] = second[d * rows : (d + 1) * rows, :]
+    swap_start(part, red, send3, recv3)
+    red[me] = part[me]
+    swap_wait(part, red, send3, recv3)
+    total = red[0]
+    for d in range(1, devices):
+        total = total + red[d]
+    mine[...] = total
+    gath[my] = total
+
+    def all_copy(other, slot):
+        return pltpu.make_async_remote_copy(
+            src_ref=mine, dst_ref=gath.at[slot], send_sem=send4.at[other], recv_sem=recv4.at[slot],
+            device_id=(lax.rem(other, devices), other // devices), device_id_type=mesh_ids,
+        )
+
+    def spread(step, carry):
+        all_copy(lax.rem(my + step, everyone), my).start()
+        return carry
+
+    def collect(step, carry):
+        other = lax.rem(my + step, everyone)
+        all_copy(other, other).wait()
+        return carry
+
+    lax.fori_loop(1, everyone, spread, 0)
+    lax.fori_loop(1, everyone, collect, 0)
+    for d in range(devices):
+        total = gath[d]
+        for c in range(1, cores):
+            total = total + gath[c * devices + d]
+        total_ref[d] = total
+
+
+def exchange_pass(states, slopes, sums, decay_rates, span):
+    devices = lax.axis_size("seq")
+    everyone = devices * lax.axis_size("ch")
+    modes, filters = decay_rates.shape
+    rows = 2 * modes // devices
+    f32 = jnp.float32
+    sem = pltpu.SemaphoreType.DMA
+    vmem = pl.BlockSpec(memory_space=pltpu.VMEM)
+    far, total = pl.pallas_call(
+        functools.partial(exchange_kernel, span),
+        in_specs=[vmem] * 4,
+        out_specs=[vmem] * 2,
+        out_shape=[
+            jax.ShapeDtypeStruct(states.shape, f32),
+            jax.ShapeDtypeStruct((devices, rows, filters), f32),
+        ],
+        scratch_shapes=[
+            pltpu.VMEM(states.shape, f32),
+            pltpu.VMEM(states.shape, f32),
+            pltpu.VMEM(states.shape, f32),
+            pltpu.VMEM((devices, rows, filters), f32),
+            pltpu.VMEM((devices, rows, filters), f32),
+            pltpu.VMEM((rows, filters), f32),
+            pltpu.VMEM((everyone, rows, filters), f32),
+        ]
+        + [sem((devices,))] * 6
+        + [sem((everyone,))] * 2,
+        compiler_params=pltpu.CompilerParams(
+            collective_id=0, has_side_effects=True, vmem_limit_bytes=60 * 1024 * 1024
+        ),
+        name="exchange_pass",
+    )(states, slopes, sums, decay_rates)
+    total = total.reshape(2, modes, filters)
+    return far, total[0], total[1]
+
+
+def plain_exchange(states, slopes, sums, decay_rates, span):
+    devices = lax.axis_size("seq")
+    me = lax.axis_index("seq")
+    groups = states.shape[0]
+    modes, filters = decay_rates.shape
+    share = groups * modes // devices
+    sent = states.transpose(0, 2, 1, 3).reshape(devices, share, 2, filters).transpose(0, 2, 1, 3)
+    received = lax.all_to_all(sent, "seq", split_axis=0, concat_axis=0, tiled=True)
+    row_rates = jnp.tile(decay_rates, (groups, 1)).reshape(devices, share, filters)
+    own_rates = lax.dynamic_index_in_dim(row_rates, me, 0, keepdims=False)
+    answer, first, second = owner_pass(received, own_rates, span)
+    far = lax.all_to_all(answer, "seq", split_axis=0, concat_axis=0, tiled=True)
+    far = far.transpose(0, 2, 1, 3).reshape(groups, modes, 2, filters).transpose(0, 2, 1, 3)
+    crossing = jnp.sum(slopes[:, 1] * far[:, 0] + slopes[:, 0] * far[:, 1], axis=0)
+    owned = jnp.zeros((2, groups * modes, filters), jnp.float32)
+    owned = lax.dynamic_update_slice(owned, jnp.stack([first, second]), (0, me * share, 0))
+    owned = owned.reshape(2, groups, modes, filters).sum(1)
+    zeroth = sums[0] + owned[0]
+    moment = sums[1] + owned[1] + crossing
+    zeroth, moment = lax.psum((zeroth, moment), ("seq", "ch"))
+    return far, zeroth, moment
+
+
 def finish_kernel(
     length, k_ref, v_ref, g_ref, wgt_ref, dec_ref, conv_ref, back_ref, hin_ref, gin_ref, far_ref,
     dq_ref, dk_ref, dv_ref, nat_ref,
@@ -293,14 +464,13 @@
         out_specs=[column] * 3,
         out_shape=[jax.ShapeDtypeStruct((rows, channels), jnp.bfloat16)] * 3,
         scratch_shapes=[pltpu.VMEM((rows, filters), jnp.float32)],
-        compiler_params=pltpu.CompilerParams(vmem_limit_bytes=32 * 1024 * 1024),
+        compiler_params=pltpu.CompilerParams(vmem_limit_bytes=60 * 1024 * 1024),
         name="finish_pass",
     )(key_in, values, cotangent, weights, decay_rates, conv, back, hin, gin, far)
 
 
 def shards(query, key_in, values, cotangent, residues, decay_rates):
     devices = lax.axis_size("seq")
-    me = lax.axis_index("seq")
     rows, channels = query.shape
     modes, filters = decay_rates.shape
     groups = channels // filters
@@ -310,20 +480,10 @@
     conv, back, hin, gin, states, slopes, sums = local_pass(
         query, key_in, values, cotangent, weights, decay_rates
     )
-    sent = states.transpose(0, 2, 1, 3).reshape(devices, share, 2, filters).transpose(0, 2, 1, 3)
-    received = lax.all_to_all(sent, "seq", split_axis=0, concat_axis=0, tiled=True)
-    row_rates = jnp.tile(decay_rates, (groups, 1)).reshape(devices, share, filters)
-    own_rates = lax.dynamic_index_in_dim(row_rates, me, 0, keepdims=False)
-    answer, first, second = owner_pass(received, own_rates, float(rows))
-    far = lax.all_to_all(answer, "seq", split_axis=0, concat_axis=0, tiled=True)
-    far = far.transpose(0, 2, 1, 3).reshape(groups, modes, 2, filters).transpose(0, 2, 1, 3)
-    crossing = jnp.sum(slopes[:, 1] * far[:, 0] + slopes[:, 0] * far[:, 1], axis=0)
-    owned = jnp.zeros((2, groups * modes, filters), jnp.float32)
-    owned = lax.dynamic_update_slice(owned, jnp.stack([first, second]), (0, me * share, 0))
-    owned = owned.reshape(2, groups, modes, filters).sum(1)
-    zeroth = sums[0] + owned[0]
-    moment = sums[1] + owned[1] + crossing
-    zeroth, moment = lax.psum((zeroth, moment), ("seq", "ch"))
+    if share == modes and modes % (devices // 2) == 0:
+        far, zeroth, moment = exchange_pass(states, slopes, sums, decay_rates, float(rows))
+    else:
+        far, zeroth, moment = plain_exchange(states, slopes, sums, decay_rates, float(rows))
     query_grad, key_grad, value_grad = finish_pass(
         key_in, values, cotangent, weights, decay_rates, conv, back, hin, gin, far
     )

time: 125 us -> 75.6 us (0.60)
  blocking collectives: 57.2 us -> 0 us
  Pallas kernels: 34.2 us -> 72.4 us
  local copies, waits for them, and re-layouts: 17.2 us -> 0.02 us
  waiting for transfers between devices: 6.19 us -> 0 us
  starting transfers between devices: 3.55 us -> 0 us
  other arithmetic: 4.67 us -> 1.97 us
    psum x1 -> x0, blocking collectives: 39 us -> none  [shards(): zeroth, moment = lax.psum((zeroth, moment), ('seq', 'ch'))]
    pallas_call x1, Pallas kernels: 1.7 us -> 34.4 us  [exchange_pass(): pl.pallas_call(functools.partial(exchange_kernel, span), in_specs=[vmem]...]
    all_to_all x1 -> x0, blocking collectives: 18.2 us -> none  [shards(): lax.all_to_all(sent, 'seq', split_axis=0, concat_axis=0, tiled=True)]
    unnamed x38 -> x6, local copies, waits for them, and re-layouts: 16.5 us -> 0.02 us
    all_to_all x1 -> x0, waiting for transfers between devices: 6.19 us -> none  [shards(): far = lax.all_to_all(answer, 'seq', split_axis=0, concat_axis=0, tiled=True)]
    pallas_call x1, Pallas kernels: 9.33 us -> 13.5 us  [finish_pass(): pl.pallas_call(functools.partial(finish_kernel, length), grid=(groups,),...]
    all_to_all x1 -> x0, starting transfers between devices: 3.55 us -> none  [shards(): far = lax.all_to_all(answer, 'seq', split_axis=0, concat_axis=0, tiled=True)]
    reduce_sum x2 -> x0, other arithmetic: 1.98 us -> none  [the longest x1 1.01 us: shards(): jnp.sum(slopes[:, 1] * far[:, 0] + slopes[:, 0] * far[:, 1], axis=0)]
  transfers between devices with their start and end apart: 1 -> 0, of which waited for: 1 -> 0; matrix products, arithmetic and copies ran while one was open for 2% -> 0% of each run, Pallas kernels for 0% -> 0%
where the time goes in v2:
time: 75.6 us; the launch traced here: 75.1 us
  Pallas kernels  72.4 us (96%)
  other arithmetic  1.97 us (3%)
    pallas_call x1, Pallas kernels, exchange_pass(): pl.pallas_call(functools.partial(exchange_kernel, span), in_specs=[vmem]...  34.4 us
    pallas_call x1, Pallas kernels, local_pass(): pl.pallas_call(functools.partial(local_kernel, length), grid=(groups,), i...  24.5 us
    pallas_call x1, Pallas kernels, finish_pass(): pl.pallas_call(functools.partial(finish_kernel, length), grid=(groups,),...  13.5 us

profile of v2, /device:TPU:0, one launch (start us, length us, event | category | flops | bytes accessed | tf_op | source)
XLA Modules:
  0.0 75.1 jit_solution(11363528884802251342)
XLA Ops:
  0.6 1.3 %fusion.wgt_ref = f32[16,128]{1,0:T(8,128)} fusion(f32[16,128]{1,0:T(8,128)} %param.10, f32[16,128]{1,0:T(8,128)} %dec_ref.5), kind=kLoop, calls=%fused_computation.3 | loop fusion | flops 6144 | bytes 24576 | tf_op jit(solution)/shard_map/mul | solution.py:479
  2.0 24.5 %local_pass.1 = (f32[16,32,8,128]{3,2,1,0:T(8,128)}, f32[16,32,8,128]{3,2,1,0:T(8,128)}, f32[16,16,8,128]{3,2,1,0:T(8,128)}, f32[16,16,8,128]{3,2,1,0:T(8,128)},...) custom-call(bf16[256,2048]{1,0:T(8,128)(2,1)} %k_ref.3, bf16[256,2048]{1,0:T(8,128)(2,1)} %v_ref.3, ...), custom_call_target="tpu_custom_call" | custom-call | tf_op jit(solution)/shard_map/local_pass/pallas_call | solution.py:182
  26.5 34.4 %exchange_pass.1 = (f32[16,2,16,128]{3,2,1,0:T(8,128)}, f32[16,2,128]{2,1,0:T(2,128)}) custom-call(f32[16,2,16,128]{3,2,1,0:T(8,128)} %get-tuple-element.21.x_ref, f32[16,2,16,128]{3,2,1,0:T(8,128)} %get-tuple-element.22.slope_ref, f32[2,16,128]{2,1,0:T(8,128)} %get-tuple-element.23.sums_ref, f32[16,128]{1,0:T(8,128)} %dec_ref.5), custom_call_target="tpu_custom_call" | custom-call | tf_op jit(solution)/shard_map/exchange_pass/pallas_call | solution.py:365
  60.9 0.0 copy-start.2
  60.9 0.0 copy-start
  60.9 0.0 copy-start.1
  60.9 13.5 %finish_pass.1 = (bf16[256,2048]{1,0:T(8,128)(2,1)}, bf16[256,2048]{1,0:T(8,128)(2,1)}, bf16[256,2048]{1,0:T(8,128)(2,1)}) custom-call(bf16[256,2048]{1,0:T(8,128)(2,1)} %k_ref.3, bf16[256,2048]{1,0:T(8,128)(2,1)} %v_ref.3, bf16[256,2048]{1,0:T(8,128)(2,1)} %g_ref.3, f32[16,128]{1,0:T(8,128)} %fusion.wgt_ref, f32[16,128]{1,0:T(8,128)} %dec_ref.5, ...), custom_call_target="tpu_custom_call" | custom-call | tf_op jit(solution)/shard_map/finish_pass/pallas_call | solution.py:460
  74.4 0.0 copy-done.2
  74.5 0.0 copy-done
  74.5 0.0 copy-done.1
  74.5 0.6 multiply_multiply_fusion
  (1 shorter events, 0.0 us)
Async XLA Ops:
  60.9 13.5 %copy-start.2 = (f32[16,2,128]{2,1,0:T(2,128)S(1)}, f32[16,2,128]{2,1,0:T(2,128)}, u32[]{:S(2)}) copy-start(f32[16,2,128]{2,1,0:T(2,128)} %get-tuple-element.28) | copy-start | bytes 49156
  60.9 13.5 %copy-start = (f32[16,128]{1,0:T(8,128)S(1)}, f32[16,128]{1,0:T(8,128)}, u32[]{:S(2)}) copy-start(f32[16,128]{1,0:T(8,128)} %dec_ref.5) | copy-start | bytes 24580
  60.9 13.5 %copy-start.1 = (f32[16,128]{1,0:T(8,128)S(1)}, f32[16,128]{1,0:T(8,128)}, u32[]{:S(2)}) copy-start(f32[16,128]{1,0:T(8,128)} %param.10) | copy-start | bytes 24580

commit v3 on v2

--- a/solution.py
+++ b/solution.py
@@ -419,32 +419,34 @@
 ):
     modes = dec_ref.shape[0]
     sub = lax.broadcasted_iota(jnp.int32, (SUBS, LANES), 0).astype(jnp.float32)
-    decay = []
-    ahead = []
-    behind = []
-    for m in range(modes):
-        rate = dec_ref[m : m + 1, :]
-        weight = wgt_ref[m : m + 1, :]
-        decay.append(wide(jnp.exp(-rate)))
-        before = jnp.exp(-rate * (sub * float(length)))
-        after = jnp.exp(-rate * ((SUBS - 1.0 - sub) * float(length)))
-        ahead.append(weight * (hin_ref[0, m] + before * far_ref[0, 0, m : m + 1, :]))
-        behind.append(weight * (gin_ref[0, m] + after * far_ref[0, 1, m : m + 1, :]))
-
     def total(parts):
         while len(parts) > 1:
             parts = [sum(parts[i : i + 2]) for i in range(0, len(parts), 2)]
         return parts[0]
 
-    for j in range(length):
-        nat_ref[pl.ds(j, SUBS, stride=length), :] = conv_ref[0, j] + total(ahead)
-        ahead = [x * a for x, a in zip(ahead, decay)]
-    dq_ref[...] = (g_ref[...].astype(jnp.float32) * nat_ref[...]).astype(jnp.bfloat16)
-    for j in reversed(range(length)):
-        behind = [x * a for x, a in zip(behind, decay)]
-        nat_ref[pl.ds(j, SUBS, stride=length), :] = back_ref[0, j] + total(behind)
-    dk_ref[...] = (v_ref[...].astype(jnp.float32) * nat_ref[...]).astype(jnp.bfloat16)
-    dv_ref[...] = (k_ref[...].astype(jnp.float32) * nat_ref[...]).astype(jnp.bfloat16)
+    for i in range(conv_ref.shape[0]):
+        cols = slice(i * LANES, (i + 1) * LANES)
+        decay = []
+        ahead = []
+        behind = []
+        for m in range(modes):
+            rate = dec_ref[m : m + 1, :]
+            weight = wgt_ref[m : m + 1, :]
+            decay.append(wide(jnp.exp(-rate)))
+            before = jnp.exp(-rate * (sub * float(length)))
+            after = jnp.exp(-rate * ((SUBS - 1.0 - sub) * float(length)))
+            ahead.append(weight * (hin_ref[i, m] + before * far_ref[i, 0, m : m + 1, :]))
+            behind.append(weight * (gin_ref[i, m] + after * far_ref[i, 1, m : m + 1, :]))
+
+        for j in range(length):
+            nat_ref[pl.ds(j, SUBS, stride=length), :] = conv_ref[i, j] + total(ahead)
+            ahead = [x * a for x, a in zip(ahead, decay)]
+        dq_ref[:, cols] = (g_ref[:, cols].astype(jnp.float32) * nat_ref[...]).astype(jnp.bfloat16)
+        for j in reversed(range(length)):
+            behind = [x * a for x, a in zip(behind, decay)]
+            nat_ref[pl.ds(j, SUBS, stride=length), :] = back_ref[i, j] + total(behind)
+        dk_ref[:, cols] = (v_ref[:, cols].astype(jnp.float32) * nat_ref[...]).astype(jnp.bfloat16)
+        dv_ref[:, cols] = (k_ref[:, cols].astype(jnp.float32) * nat_ref[...]).astype(jnp.bfloat16)
 
 
 def finish_pass(key_in, values, cotangent, weights, decay_rates, conv, back, hin, gin, far):
@@ -452,14 +454,15 @@
     modes, filters = decay_rates.shape
     groups = channels // filters
     length = rows // SUBS
-    column = pl.BlockSpec((rows, filters), lambda g: (0, g))
+    per = 2 if groups % 2 == 0 else 1
+    column = pl.BlockSpec((rows, per * filters), lambda g: (0, g))
     small = pl.BlockSpec((modes, filters), lambda g: (0, 0))
-    piece = pl.BlockSpec((1, length, SUBS, filters), lambda g: (g, 0, 0, 0))
-    inner = pl.BlockSpec((1, modes, SUBS, filters), lambda g: (g, 0, 0, 0))
-    pair = pl.BlockSpec((1, 2, modes, filters), lambda g: (g, 0, 0, 0))
+    piece = pl.BlockSpec((per, length, SUBS, filters), lambda g: (g, 0, 0, 0))
+    inner = pl.BlockSpec((per, modes, SUBS, filters), lambda g: (g, 0, 0, 0))
+    pair = pl.BlockSpec((per, 2, modes, filters), lambda g: (g, 0, 0, 0))
     return pl.pallas_call(
         functools.partial(finish_kernel, length),
-        grid=(groups,),
+        grid=(groups // per,),
         in_specs=[column] * 3 + [small] * 2 + [piece, piece, inner, inner, pair],
         out_specs=[column] * 3,
         out_shape=[jax.ShapeDtypeStruct((rows, channels), jnp.bfloat16)] * 3,

time: 75.6 us -> 72.4 us (0.958)
  Pallas kernels: 72.4 us -> 69.3 us
    pallas_call x1, Pallas kernels: 13.5 us -> 10.4 us  [finish_pass(): pl.pallas_call(functools.partial(finish_kernel, length), grid=(groups //...]
where the time goes in v3:
time: 72.4 us; the launch traced here: 72 us
  Pallas kernels  69.3 us (96%)
  other arithmetic  1.97 us (3%)
    pallas_call x1, Pallas kernels, exchange_pass(): pl.pallas_call(functools.partial(exchange_kernel, span), in_specs=[vmem]...  34.4 us
    pallas_call x1, Pallas kernels, local_pass(): pl.pallas_call(functools.partial(local_kernel, length), grid=(groups,), i...  24.5 us
    pallas_call x1, Pallas kernels, finish_pass(): pl.pallas_call(functools.partial(finish_kernel, length), grid=(groups //...  10.4 us

profile of v3, /device:TPU:0, one launch (start us, length us, event | category | flops | bytes accessed | tf_op | source)
XLA Modules:
  0.0 72.0 jit_solution(15539233083013540300)
XLA Ops:
  0.6 1.3 %fusion.wgt_ref = f32[16,128]{1,0:T(8,128)} fusion(f32[16,128]{1,0:T(8,128)} %param.10, f32[16,128]{1,0:T(8,128)} %dec_ref.5), kind=kLoop, calls=%fused_computation.3 | loop fusion | flops 6144 | bytes 24576 | tf_op jit(solution)/shard_map/mul | solution.py:482
  2.0 24.5 %local_pass.1 = (f32[16,32,8,128]{3,2,1,0:T(8,128)}, f32[16,32,8,128]{3,2,1,0:T(8,128)}, f32[16,16,8,128]{3,2,1,0:T(8,128)}, f32[16,16,8,128]{3,2,1,0:T(8,128)},...) custom-call(bf16[256,2048]{1,0:T(8,128)(2,1)} %k_ref.3, bf16[256,2048]{1,0:T(8,128)(2,1)} %v_ref.3, ...), custom_call_target="tpu_custom_call" | custom-call | tf_op jit(solution)/shard_map/local_pass/pallas_call | solution.py:182
  26.5 34.4 %exchange_pass.1 = (f32[16,2,16,128]{3,2,1,0:T(8,128)}, f32[16,2,128]{2,1,0:T(2,128)}) custom-call(f32[16,2,16,128]{3,2,1,0:T(8,128)} %get-tuple-element.21.x_ref, f32[16,2,16,128]{3,2,1,0:T(8,128)} %get-tuple-element.22.slope_ref, f32[2,16,128]{2,1,0:T(8,128)} %get-tuple-element.23.sums_ref, f32[16,128]{1,0:T(8,128)} %dec_ref.5), custom_call_target="tpu_custom_call" | custom-call | tf_op jit(solution)/shard_map/exchange_pass/pallas_call | solution.py:365
  60.9 0.0 copy-start.2
  60.9 0.0 copy-start
  60.9 0.0 copy-start.1
  60.9 10.4 %finish_pass.1 = (bf16[256,2048]{1,0:T(8,128)(2,1)}, bf16[256,2048]{1,0:T(8,128)(2,1)}, bf16[256,2048]{1,0:T(8,128)(2,1)}) custom-call(bf16[256,2048]{1,0:T(8,128)(2,1)} %k_ref.3, bf16[256,2048]{1,0:T(8,128)(2,1)} %v_ref.3, bf16[256,2048]{1,0:T(8,128)(2,1)} %g_ref.3, f32[16,128]{1,0:T(8,128)} %fusion.wgt_ref, f32[16,128]{1,0:T(8,128)} %dec_ref.5, ...), custom_call_target="tpu_custom_call" | custom-call | tf_op jit(solution)/shard_map/finish_pass/pallas_call | solution.py:463
  71.3 0.0 copy-done.2
  71.4 0.0 copy-done
  71.4 0.0 copy-done.1
  71.4 0.6 multiply_multiply_fusion
  (1 shorter events, 0.0 us)
Async XLA Ops:
  60.9 10.4 %copy-start.2 = (f32[16,2,128]{2,1,0:T(2,128)S(1)}, f32[16,2,128]{2,1,0:T(2,128)}, u32[]{:S(2)}) copy-start(f32[16,2,128]{2,1,0:T(2,128)} %get-tuple-element.28) | copy-start | bytes 49156
  60.9 10.4 %copy-start = (f32[16,128]{1,0:T(8,128)S(1)}, f32[16,128]{1,0:T(8,128)}, u32[]{:S(2)}) copy-start(f32[16,128]{1,0:T(8,128)} %dec_ref.5) | copy-start | bytes 24580
  60.9 10.4 %copy-start.1 = (f32[16,128]{1,0:T(8,128)S(1)}, f32[16,128]{1,0:T(8,128)}, u32[]{:S(2)}) copy-start(f32[16,128]{1,0:T(8,128)} %param.10) | copy-start | bytes 24580
